TPU v7x, 768 devices: a whole 4x8x12 slice. The times are simulated.
768 devices in a mesh: grp: 48 (over z, x), mem: 16 (over y, core).
Axes of the slice: x: 4, y: 8, z: 12, core: 2. Of those that a mesh axis runs over, the one named last changes fastest.
Arguments:
- source_rows: bfloat16 [393216, 256], P(('grp', 'mem')), may hold values from -6 to 6
- source_degree: int32 [393216], P(('grp', 'mem')), may hold values from 1 to 32
- edge_tiles: int32 [24576, 128, 128], P(('grp', 'mem')), may hold values 0 or 1
- tile_row: int32 [24576], P(('grp', 'mem')), may hold values from 0 to 7
- tile_col: int32 [24576], P(('grp', 'mem')), may hold values from 0 to 3
- mirror_ids: int32 [786432], P(('grp', 'mem')), may hold values from 0 to 24575, as said below
- master_rows: bfloat16 [24576, 256], P(('grp', 'mem')), may hold values from -6 to 6
- master_degree: int32 [24576], P(('grp', 'mem')), may hold values from 64 to 1024
- weight_one: bfloat16 [256, 256], replicated, may hold values from -0.375 to 0.375
- weight_two: bfloat16 [256, 256], replicated, may hold values from -0.375 to 0.375
Outputs:
- new_master: bfloat16 [24576, 256], P(('grp', 'mem'))
- mirror_out: bfloat16 [786432, 256], P(('grp', 'mem'))
Inputs may be any that keep to these rules, and one draw needn't show every extreme that they name: `mirror_ids`: entry j of a device's 1024 entries names a vertex whose owning device has mem index j // 64; vertex v is owned by device v // 32, devices counted grp first then mem.
All inputs are finite; a program needn't handle non-finite values. No bound on the sum of `edge_tiles` on one device may be relied on, other than what follows from the above.
Results may differ from a plain program's by a relative error of at most 0.0053.
Values may be sent and summed in bfloat16 or wider, within the bound.
A program may use at most 32 MiB of HBM per device.

v0:
```python
import jax
import jax.numpy as jnp
from jax import lax
from jax.sharding import PartitionSpec as P


def update_rows(summed, rows_in, degree, weight_one, weight_two):
    neigh = summed * lax.rsqrt(degree.astype(jnp.float32))[:, None]
    embed = rows_in.astype(jnp.float32)
    first = (embed + neigh).astype(jnp.bfloat16)
    second = (neigh * embed).astype(jnp.bfloat16)
    result = jnp.dot(first, weight_one, preferred_element_type=jnp.float32) + jnp.dot(
        second, weight_two, preferred_element_type=jnp.float32
    )
    return jnp.where(result > 0, result, 0.2 * result).astype(jnp.bfloat16)


def body(
    source_rows,
    source_degree,
    edge_tiles,
    tile_row,
    tile_col,
    mirror_ids,
    master_rows,
    master_degree,
    weight_one,
    weight_two,
):
    tile_size = edge_tiles.shape[1]
    width = source_rows.shape[1]
    group_count = lax.axis_size("grp")
    owned = master_rows.shape[0]
    member_count = lax.axis_size("mem")
    slot_total = mirror_ids.shape[0]
    scaled = (
        source_rows.astype(jnp.float32) * lax.rsqrt(source_degree.astype(jnp.float32))[:, None]
    ).astype(jnp.bfloat16)
    blocks = scaled.reshape(-1, tile_size, width)
    picked = blocks[tile_col]
    products = jnp.einsum(
        "trc,tcd->trd", edge_tiles.astype(jnp.bfloat16), picked, preferred_element_type=jnp.float32
    )
    onehot = (
        tile_row[:, None] == jnp.arange(slot_total // tile_size, dtype=jnp.int32)[None, :]
    ).astype(jnp.float32)
    partial_value = jnp.einsum(
        "tb,trd->brd", onehot, products, precision=lax.Precision.HIGHEST
    ).reshape(slot_total, width)
    received, got_ids = (
        lax.all_to_all(partial_value, "mem", split_axis=0, concat_axis=0, tiled=True),
        lax.all_to_all(mirror_ids, "mem", split_axis=0, concat_axis=0, tiled=True),
    )
    owner_dev = got_ids // owned
    local_index = owner_dev // member_count * owned + got_ids % owned
    column = jax.ops.segment_sum(received, local_index, num_segments=group_count * owned)
    shares = lax.psum_scatter(column, "grp", scatter_dimension=0, tiled=True)
    new_master = update_rows(shares, master_rows, master_degree, weight_one, weight_two)
    column_new = lax.all_gather(new_master, "grp", axis=0, tiled=True)
    served = column_new[local_index]
    mirror_out = lax.all_to_all(served, "mem", split_axis=0, concat_axis=0, tiled=True)
    return (new_master, mirror_out)


def solution(mesh):
    in_specs = (
        P(("grp", "mem"), None),
        P(("grp", "mem")),
        P(("grp", "mem"), None, None),
        P(("grp", "mem")),
        P(("grp", "mem")),
        P(("grp", "mem")),
        P(("grp", "mem"), None),
        P(("grp", "mem")),
        P(),
        P(),
    )
    out_specs = (P(("grp", "mem"), None), P(("grp", "mem"), None))
    return jax.shard_map(body, mesh=mesh, in_specs=in_specs, out_specs=out_specs, check_vma=False)
```

profile of v0, /device:TPU:1, one launch (start us, length us, event | category | flops | bytes accessed | tf_op | source)
XLA Modules:
  0.0 620.9 jit_solution(4717938811543167359)
XLA Ops:
  7.2 0.0 copy-start
  7.2 1.4 all_to_all.24
  8.6 13.8 %all-to-all-start = ((s32[16,64,1]{1,2,0:T(1,128)}), s32[16,64,1]{1,2,0:T(1,128)S(1)}, u32[]{:S(2)}, u32[]{:S(2)}) async-start(s32[16,64,1]{1,2,0:T(1,128)} %bitcast), calls=%async_computation | async-start | bytes 16384 | tf_op jit(solution)/shard_map/all_to_all | solution.py:52
  22.3 0.7 convert_rsqrt_fusion
  23.0 0.7 compare_select_fusion.8
  23.7 1.1 multiply_convert_fusion
  24.8 0.7 gather_fusion
  25.5 4.3 convolution_bitcast_fusion
  29.8 0.0 copy-start.4
  29.8 5.5 copy.18
  35.3 0.0 copy-done.4
  35.3 3.6 fusion.13
  38.9 1.3 copy.19
  40.2 0.0 all-to-all-done
  40.2 7.3 %all-to-all-start.1 = ((f32[16,64,256]{2,1,0:T(8,128)}), f32[16,64,256]{2,1,0:T(8,128)S(1)}, u32[]{:S(2)}, u32[]{:S(2)}) async-start(f32[16,64,256]{2,1,0:T(8,128)} %bitcast.5), calls=%async_computation.1 | async-start | bytes 2097152 | tf_op jit(solution)/shard_map/all_to_all | solution.py:51
  47.5 0.0 copy-start.5
  47.5 0.0 copy-start.3
  47.5 0.0 copy-start.1
  47.5 0.0 reduce-scatter.2.cloned.1.call-start
  47.6 0.5 broadcast.229
  48.1 0.7 reduce.3
  48.8 0.1 all_to_all.26
  48.8 0.1 compare_select_fusion.1
  48.9 26.5 %all-to-all-done.1 = f32[16,64,256]{2,1,0:T(8,128)S(1)} async-done(((f32[16,64,256]{2,1,0:T(8,128)}), f32[16,64,256]{2,1,0:T(8,128)S(1)}, u32[]{:S(2)}, u32[]{:S(2)}) %all-to-all-start.1) | async-done | bytes 1048608 | tf_op jit(solution)/shard_map/all_to_all | solution.py:51
  75.4 7.3 %scatter_custom_fusion = f32[1536,256]{1,0:T(8,128)} fusion(s32[1024]{0:T(1024)S(1)} %bitcast.23, f32[1024,256]{1,0:T(8,128)S(1)} %bitcast.21, f32[]{:T(128)} %constant.39.clone.1), kind=kCustom, calls=%fused_computation.6 | custom fusion | flops 262144 | bytes 1572868 | tf_op jit(solution)/shard_map/scatter-add | solution.py:56
  82.7 0.0 reduce-scatter.2.cloned.1.call-update
  82.7 0.0 copy-done.5
  82.7 417.9 %reduce-scatter.2.cloned.1.call-done = f32[32,256]{1,0:T(8,128)} async-done(((f32[1536,256]{1,0:T(8,128)}), f32[32,256]{1,0:T(8,128)}) %reduce-scatter.2.cloned.1.call-update) | async-done | bytes 32784 | tf_op jit(solution)/shard_map/reduce_scatter | solution.py:57
  500.7 0.0 copy-done
  500.7 0.0 copy-done.3
  500.7 0.9 fusion.7
  501.6 0.0 copy-done.1
  501.6 1.0 fusion.3
  502.6 0.0 copy-start.2
  502.6 56.1 %all_gather.3 = bf16[1536,256]{1,0:T(8,128)(2,1)S(1)} all-gather(bf16[32,256]{1,0:T(8,128)(2,1)S(1)} %fusion.3), channel_id=1, replica_groups=mesh['grp'=48,'mem'=16] {'grp'}, dimensions={0}, use_global_device_ids=true | all-gather | bytes 802816 | tf_op jit(solution)/shard_map/all_gather | solution.py:59
  558.6 3.9 gather_fusion.1
  562.6 0.0 copy-done.2
  562.6 50.6 %all_to_all.36 = bf16[16,64,256]{2,1,0:T(8,128)(2,1)S(1)} all-to-all(bf16[16,64,256]{2,1,0:T(8,128)(2,1)S(1)} %bitcast.20), channel_id=1, replica_groups=mesh['grp'=48,'mem'=16] {'mem'}, dimensions={0} | all-to-all | bytes 1048576 | tf_op jit(solution)/shard_map/all_to_all | solution.py:61
  613.2 0.8 copy.22
  (3 shorter events, 0.0 us)
Async XLA Ops:
  7.2 493.5 %copy-start = (bf16[256,256]{1,0:T(8,128)(2,1)S(1)}, bf16[256,256]{1,0:T(8,128)(2,1)}, u32[]{:S(2)}) copy-start(bf16[256,256]{1,0:T(8,128)(2,1)} %param.18) | copy-start | bytes 393220
  8.6 31.6 %all-to-all-start = ((s32[16,64,1]{1,2,0:T(1,128)}), s32[16,64,1]{1,2,0:T(1,128)S(1)}, u32[]{:S(2)}, u32[]{:S(2)}) async-start(s32[16,64,1]{1,2,0:T(1,128)} %bitcast), calls=%async_computation | async-start | bytes 16384 | tf_op jit(solution)/shard_map/all_to_all | solution.py:52
  29.8 5.5 copy-start.4
  40.2 35.2 %all-to-all-start.1 = ((f32[16,64,256]{2,1,0:T(8,128)}), f32[16,64,256]{2,1,0:T(8,128)S(1)}, u32[]{:S(2)}, u32[]{:S(2)}) async-start(f32[16,64,256]{2,1,0:T(8,128)} %bitcast.5), calls=%async_computation.1 | async-start | bytes 2097152 | tf_op jit(solution)/shard_map/all_to_all | solution.py:51
  47.5 35.2 %copy-start.5 = (s32[32]{0:T(128)S(1)}, s32[32]{0:T(128)}, u32[]{:S(2)}) copy-start(s32[32]{0:T(128)} %param.17) | copy-start | bytes 388
  47.5 453.2 %copy-start.3 = (bf16[32,256]{1,0:T(8,128)(2,1)S(1)}, bf16[32,256]{1,0:T(8,128)(2,1)}, u32[]{:S(2)}) copy-start(bf16[32,256]{1,0:T(8,128)(2,1)} %param.16) | copy-start | bytes 49156
  47.5 454.1 %copy-start.1 = (bf16[256,256]{1,0:T(8,128)(2,1)S(1)}, bf16[256,256]{1,0:T(8,128)(2,1)}, u32[]{:S(2)}) copy-start(bf16[256,256]{1,0:T(8,128)(2,1)} %param.19) | copy-start | bytes 393220
  47.5 453.1 %reduce-scatter.2.cloned.1.call-start = ((), (), s32[]{:S(2)}) async-start(), calls=%async_computation.4 | async-start | bytes 1605632 | tf_op jit(solution)/shard_map/reduce_scatter | solution.py:57
  502.6 60.0 %copy-start.2 = (bf16[32,256]{1,0:T(8,128)(2,1)}, bf16[32,256]{1,0:T(8,128)(2,1)S(1)}, u32[]{:S(2)}) copy-start(bf16[32,256]{1,0:T(8,128)(2,1)S(1)} %fusion.3) | copy-start | bytes 49156
Sparse Core Ops, SparseCore 0:
  82.8 417.8 reduce-scatter.1
where the time goes:
time: 622 us; the launch traced here: 621 us
  waiting for transfers between devices  444 us (71%)
  blocking collectives  107 us (17%)
  starting transfers between devices  21.1 us (3%)
  local copies, waits for them, and re-layouts  14.2 us (2%)
  between operations  14.1 us (2%)
  other arithmetic  10.4 us (2%)
  matrix products  9.81 us (2%)
    reduce_scatter x1, waiting for transfers between devices, body(): shares = lax.psum_scatter(column, 'grp', scatter_dimension=0, tiled=True)  418 us
    all_gather x1, blocking collectives, body(): column_new = lax.all_gather(new_master, 'grp', axis=0, tiled=True)  56.1 us
    all_to_all x1, blocking collectives, body(): lax.all_to_all(served, 'mem', split_axis=0, concat_axis=0, tiled=True)  50.6 us
    all_to_all x1, waiting for transfers between devices, body(): lax.all_to_all(partial_value, 'mem', split_axis=0, concat_axis=0, tiled=T...  26.5 us
    all_to_all x1, starting transfers between devices, body(): lax.all_to_all(mirror_ids, 'mem', split_axis=0, concat_axis=0, tiled=True)  13.8 us
  transfers between devices with their start and end apart: 3, of which 2 were waited for; matrix products, arithmetic and copies ran while one was open for 3% of the time, Pallas kernels for 0%

commit v1 on v0

v1 whole, which is shorter than its diff:
```python
import functools

import jax
import jax.numpy as jnp
from jax import lax
from jax.experimental import pallas as pl
from jax.experimental.pallas import tpu as pltpu
from jax.sharding import PartitionSpec as P

MESH = pl.DeviceIdType.MESH
NX = 4
LANE = 128
HALVES = 2


def local_kernel(trow, tcol, src, deg, tiles, out, scaled, acc):
    tile = tiles.shape[1]
    n_tiles = tiles.shape[0]
    scale = lax.rsqrt(deg[...].astype(jnp.float32))
    for k in range(src.shape[0] // tile):
        column = jnp.broadcast_to(scale[k : k + 1, :], (tile, tile)).T
        rows = pl.ds(k * tile, tile)
        for h in range(HALVES):
            cols = pl.ds(h * LANE, LANE)
            scaled[rows, cols] = (src[rows, cols].astype(jnp.float32) * column).astype(jnp.bfloat16)
    acc[...] = jnp.zeros_like(acc)

    def one(t, carry):
        r = pl.multiple_of(trow[t] * tile, tile)
        c = pl.multiple_of(tcol[t] * tile, tile)
        edges = tiles[t].astype(jnp.float32).astype(jnp.bfloat16)
        acc[pl.ds(r, tile), :] += jnp.dot(
            edges, scaled[pl.ds(c, tile), :], preferred_element_type=jnp.float32
        )
        return carry

    lax.fori_loop(0, n_tiles, one, 0, unroll=4)
    for h in range(HALVES):
        out[h] = acc[:, h * LANE : (h + 1) * LANE].astype(jnp.bfloat16)


def exchange_kernel(
    n_grp, n_mem, part, ids, mrow, mdeg, w1, w2, newm, mirror,
    precv, idrecv, idrow, put, take, col, xacc, xrecv, zsend, zrecv, colnew, served,
    id_s, id_r, y_s, y_r, x_s, x_r, z_s, z_r, gz_s, gz_r, gx_s, gx_r, b_s, b_r,
):
    g = lax.axis_index("grp")
    m = lax.axis_index("mem")
    n_z = n_grp // NX
    x = lax.rem(g, NX)
    z = g // NX
    slots = part.shape[1] // n_mem
    owned = mrow.shape[0]
    xrows = n_z * owned

    def at_mem(k):
        return lax.rem(m + k, n_mem)

    def at_x(k):
        return lax.rem(x + k, NX)

    def at_z(k):
        return lax.rem(z + k, n_z)

    barrier = pltpu.get_barrier_semaphore()

    def hello_mem(k, carry):
        pl.semaphore_signal(barrier, inc=1, device_id=(g, at_mem(k)), device_id_type=MESH)
        return carry

    def hello_x(k, carry):
        pl.semaphore_signal(barrier, inc=1, device_id=(z * NX + at_x(k), m), device_id_type=MESH)
        return carry

    def hello_z(k, carry):
        pl.semaphore_signal(barrier, inc=1, device_id=(at_z(k) * NX + x, m), device_id_type=MESH)
        return carry

    lax.fori_loop(1, n_mem, hello_mem, 0)
    lax.fori_loop(1, NX, hello_x, 0)
    lax.fori_loop(1, n_z, hello_z, 0)
    pl.semaphore_wait(barrier, (n_mem - 1) + (NX - 1) + (n_z - 1))

    def each(count, fn):
        def body(k, carry):
            fn(k)
            return carry

        lax.fori_loop(1, count, body, 0)

    def id_copy(to, who):
        return pltpu.make_async_remote_copy(
            src_ref=ids.at[to], dst_ref=idrecv.at[who], send_sem=id_s.at[to], recv_sem=id_r.at[who],
            device_id=(g, to), device_id_type=MESH)

    def y_copy(h, to, who):
        return pltpu.make_async_remote_copy(
            src_ref=part.at[h, pl.ds(to * slots, slots)], dst_ref=precv.at[h, pl.ds(who * slots, slots)],
            send_sem=y_s.at[h, to], recv_sem=y_r.at[h, who], device_id=(g, to), device_id_type=MESH)

    def x_copy(h, to, who):
        return pltpu.make_async_remote_copy(
            src_ref=col.at[h, to], dst_ref=xrecv.at[h, who], send_sem=x_s.at[h, to], recv_sem=x_r.at[h, who],
            device_id=(z * NX + to, m), device_id_type=MESH)

    def z_copy(h, to, who):
        return pltpu.make_async_remote_copy(
            src_ref=zsend.at[h, pl.ds(to * owned, owned)], dst_ref=zrecv.at[h, who],
            send_sem=z_s.at[h, to], recv_sem=z_r.at[h, who], device_id=(to * NX + x, m), device_id_type=MESH)

    def gz_copy(to, who):
        block = colnew.at[:, x, pl.ds(who * owned, owned)]
        return pltpu.make_async_remote_copy(
            src_ref=block, dst_ref=block, send_sem=gz_s.at[to], recv_sem=gz_r.at[who],
            device_id=(to * NX + x, m), device_id_type=MESH)

    def gx_copy(h, to, who):
        block = colnew.at[h, who]
        return pltpu.make_async_remote_copy(
            src_ref=block, dst_ref=block, send_sem=gx_s.at[h, to], recv_sem=gx_r.at[h, who],
            device_id=(z * NX + to, m), device_id_type=MESH)

    def b_copy(h, to, who):
        return pltpu.make_async_remote_copy(
            src_ref=served.at[h, pl.ds(to * slots, slots)],
            dst_ref=mirror.at[pl.ds(who * slots, slots), pl.ds(h * LANE, LANE)],
            send_sem=b_s.at[h, to], recv_sem=b_r.at[h, who], device_id=(g, to), device_id_type=MESH)

    each(n_mem, lambda k: id_copy(at_mem(k), m).start())
    for h in range(HALVES):
        each(n_mem, lambda k: y_copy(h, at_mem(k), m).start())
    idrecv[m] = ids[m]
    mine = pl.ds(pl.multiple_of(m * slots, slots), slots)
    for h in range(HALVES):
        precv[h, mine, :] = part[h, mine, :]
    each(n_mem, lambda k: id_copy(m, at_mem(k)).wait_recv())

    for k in range(n_mem * slots // LANE):
        lane = lax.broadcasted_iota(jnp.int32, (8, LANE), 1)
        idrow[:, k * LANE : (k + 1) * LANE] = jnp.where(lane < slots, idrecv[2 * k], idrecv[2 * k + 1])

    def build_put(q, carry):
        rows = lax.broadcasted_iota(jnp.int32, (LANE, n_mem * slots), 0) + q * LANE
        put[pl.ds(pl.multiple_of(q * LANE, LANE), LANE), :] = jnp.where(
            rows == idrow[0:1, :], 1.0, 0.0).astype(jnp.bfloat16)
        return carry

    lax.fori_loop(0, NX * xrows // LANE, build_put, 0)

    def build_take(k, carry):
        at = pl.ds(pl.multiple_of(k * LANE, LANE), LANE)
        column = jnp.broadcast_to(idrow[0:1, at], (LANE, LANE)).T
        for q in range(NX * xrows // LANE):
            lane = lax.broadcasted_iota(jnp.int32, (LANE, LANE), 1) + q * LANE
            take[at, q * LANE : (q + 1) * LANE] = jnp.where(column == lane, 1.0, 0.0).astype(jnp.bfloat16)
        return carry

    for h in range(HALVES):
        each(n_mem, lambda k: y_copy(h, m, at_mem(k)).wait_recv())
        for k in (2, 1, 3, 0):
            to = at_x(k)
            block = jnp.dot(
                put[pl.ds(pl.multiple_of(to * xrows, xrows), xrows), :], precv[h],
                preferred_element_type=jnp.float32)
            if k:
                col[h, to] = block.astype(jnp.bfloat16)
                x_copy(h, to, x).start()
            else:
                xacc[h] = block
    lax.fori_loop(0, n_mem * slots // LANE, build_take, 0)

    for h in range(HALVES):
        each(NX, lambda k: x_copy(h, x, at_x(k)).wait_recv())
        total = xacc[h]
        for k in range(1, NX):
            total = total + xrecv[h, at_x(k)].astype(jnp.float32)
        xacc[h] = total
        zsend[h] = total.astype(jnp.bfloat16)
        each(n_z, lambda k: z_copy(h, at_z(k), z).start())

    own = pl.ds(pl.multiple_of(z * owned, owned), owned)
    sums = []
    for h in range(HALVES):
        zrecv[h, z] = jnp.zeros((owned, LANE), jnp.bfloat16)
        each(n_z, lambda k: z_copy(h, z, at_z(k)).wait_recv())
        total = xacc[h, own, :]
        for k in range(n_z):
            total = total + zrecv[h, k].astype(jnp.float32)
        sums.append(total)

    scale = lax.rsqrt(mdeg[...].astype(jnp.float32))
    diagonal = lax.broadcasted_iota(jnp.int32, (owned, owned), 0) == lax.broadcasted_iota(
        jnp.int32, (owned, owned), 1)
    scale = jnp.sum(jnp.where(diagonal, jnp.broadcast_to(scale, (owned, owned)), 0.0), axis=1, keepdims=True)
    neigh = jnp.concatenate(sums, axis=1) * scale
    embed = mrow[...].astype(jnp.float32)
    first = (embed + neigh).astype(jnp.bfloat16)
    second = (neigh * embed).astype(jnp.bfloat16)
    result = jnp.dot(first, w1[...], preferred_element_type=jnp.float32) + jnp.dot(
        second, w2[...], preferred_element_type=jnp.float32)
    new = jnp.where(result > 0, result, 0.2 * result).astype(jnp.bfloat16)
    newm[...] = new
    for h in range(HALVES):
        colnew[h, x, own, :] = new[:, h * LANE : (h + 1) * LANE]

    each(n_z, lambda k: gz_copy(at_z(k), z).start())
    each(n_z, lambda k: gz_copy(z, at_z(k)).wait_recv())
    for h in range(HALVES):
        for k in (2, 1, 3):
            gx_copy(h, at_x(k), x).start()
    for h in range(HALVES):
        each(NX, lambda k: gx_copy(h, x, at_x(k)).wait_recv())
        table = colnew[h].reshape(NX * xrows, LANE)
        served[h] = jnp.dot(take[...], table, preferred_element_type=jnp.float32).astype(jnp.bfloat16)
        each(n_mem, lambda k: b_copy(h, at_mem(k), m).start())
        mirror[mine, h * LANE : (h + 1) * LANE] = served[h, mine, :]

    each(n_mem, lambda k: id_copy(at_mem(k), m).wait_send())
    for h in range(HALVES):
        each(n_mem, lambda k: y_copy(h, at_mem(k), m).wait_send())
        each(NX, lambda k: x_copy(h, at_x(k), x).wait_send())
        each(n_z, lambda k: z_copy(h, at_z(k), z).wait_send())
        each(NX, lambda k: gx_copy(h, at_x(k), x).wait_send())
    each(n_z, lambda k: gz_copy(at_z(k), z).wait_send())
    for h in range(HALVES):
        each(n_mem, lambda k: b_copy(h, m, at_mem(k)).wait_recv())
        each(n_mem, lambda k: b_copy(h, at_mem(k), m).wait_send())


def body(n_grp, n_mem, source_rows, source_degree, edge_tiles, tile_row, tile_col, mirror_ids,
         master_rows, master_degree, weight_one, weight_two):
    n_tiles, tile, _ = edge_tiles.shape
    src_dev, width = source_rows.shape
    slot_total = mirror_ids.shape[0]
    slots = slot_total // n_mem
    owned = master_rows.shape[0]
    n_z = n_grp // NX
    xrows = n_z * owned
    vmem = pl.BlockSpec(memory_space=pltpu.VMEM)
    smem = pl.BlockSpec(memory_space=pltpu.SMEM)
    bf, f32, i32 = jnp.bfloat16, jnp.float32, jnp.int32

    part = pl.pallas_call(
        local_kernel,
        out_shape=jax.ShapeDtypeStruct((HALVES, slot_total, LANE), bf),
        in_specs=[smem, smem, vmem, vmem, vmem],
        out_specs=vmem,
        scratch_shapes=[pltpu.VMEM((src_dev, width), bf), pltpu.VMEM((slot_total, width), f32)],
        compiler_params=pltpu.CompilerParams(vmem_limit_bytes=24 * 2**20),
        name="local_sums",
    )(tile_row, tile_col, source_rows, source_degree.reshape(-1, tile), edge_tiles)

    group = mirror_ids // (owned * n_mem)
    place = lax.rem(group, NX) * xrows + (group // NX) * owned + lax.rem(mirror_ids, owned)
    place = place.reshape(n_mem, 1, slots)
    ids = jnp.broadcast_to(jnp.concatenate([place, place], axis=2), (n_mem, 8, 2 * slots))

    dma = pltpu.SemaphoreType.DMA
    return pl.pallas_call(
        functools.partial(exchange_kernel, n_grp, n_mem),
        out_shape=(
            jax.ShapeDtypeStruct((owned, width), bf),
            jax.ShapeDtypeStruct((slot_total, width), bf),
        ),
        in_specs=[vmem] * 6,
        out_specs=(vmem, vmem),
        scratch_shapes=[
            pltpu.VMEM((HALVES, slot_total, LANE), bf),
            pltpu.VMEM((n_mem, 8, LANE), i32),
            pltpu.VMEM((8, slot_total), i32),
            pltpu.VMEM((NX * xrows, slot_total), bf),
            pltpu.VMEM((slot_total, NX * xrows), bf),
            pltpu.VMEM((HALVES, NX, xrows, LANE), bf),
            pltpu.VMEM((HALVES, xrows, LANE), f32),
            pltpu.VMEM((HALVES, NX, xrows, LANE), bf),
            pltpu.VMEM((HALVES, xrows, LANE), bf),
            pltpu.VMEM((HALVES, n_z, owned, LANE), bf),
            pltpu.VMEM((HALVES, NX, xrows, LANE), bf),
            pltpu.VMEM((HALVES, slot_total, LANE), bf),
            dma((n_mem,)), dma((n_mem,)),
            dma((HALVES, n_mem)), dma((HALVES, n_mem)),
            dma((HALVES, NX)), dma((HALVES, NX)),
            dma((HALVES, n_z)), dma((HALVES, n_z)),
            dma((n_z,)), dma((n_z,)),
            dma((HALVES, NX)), dma((HALVES, NX)),
            dma((HALVES, n_mem)), dma((HALVES, n_mem)),
        ],
        compiler_params=pltpu.CompilerParams(
            collective_id=0, has_side_effects=True, vmem_limit_bytes=40 * 2**20),
        name="exchange",
    )(part, ids, master_rows, master_degree.reshape(1, owned), weight_one, weight_two)


def solution(mesh):
    both = ("grp", "mem")
    in_specs = (
        P(both, None), P(both), P(both, None, None), P(both), P(both), P(both),
        P(both, None), P(both), P(), P(),
    )
    out_specs = (P(both, None), P(both, None))
    fn = functools.partial(body, mesh.shape["grp"], mesh.shape["mem"])
    return jax.shard_map(fn, mesh=mesh, in_specs=in_specs, out_specs=out_specs, check_vma=False)
```

time: 622 us -> 92.4 us (0.15)
  waiting for transfers between devices: 444 us -> 0 us
  blocking collectives: 107 us -> 0 us
  Pallas kernels: 0 us -> 84.6 us
  starting transfers between devices: 21.1 us -> 0 us
  between operations: 14.1 us -> 0.71 us
  matrix products: 9.81 us -> 0 us
  other arithmetic: 10.4 us -> 0.79 us
  local copies, waits for them, and re-layouts: 14.2 us -> 6.02 us
    reduce_scatter x1 -> x0, waiting for transfers between devices: 418 us -> none  [body(): shares = lax.psum_scatter(column, 'grp', scatter_dimension=0, tiled=True)]
    pallas_call x0 -> x2, Pallas kernels: none -> 84.6 us  [the longest x1 81.9 us: body(): pl.pallas_call(functools.partial(exchange_kernel, n_grp, n_mem), out_shap...]
    all_gather x1 -> x0, blocking collectives: 56.1 us -> none  [body(): column_new = lax.all_gather(new_master, 'grp', axis=0, tiled=True)]
    all_to_all x1 -> x0, blocking collectives: 50.6 us -> none  [body(): lax.all_to_all(served, 'mem', split_axis=0, concat_axis=0, tiled=True)]
    all_to_all x2 -> x0, waiting for transfers between devices: 26.5 us -> none  [the longest x1 26.5 us: body(): lax.all_to_all(partial_value, 'mem', split_axis=0, concat_axis=0, tiled=T...]
    all_to_all x2 -> x0, starting transfers between devices: 21 us -> none  [the longest x1 13.8 us: body(): lax.all_to_all(mirror_ids, 'mem', split_axis=0, concat_axis=0, tiled=True)]
    dot_general x4 -> x0, matrix products: 9.81 us -> none  [the longest x1 4.28 us: body(): jnp.einsum('trc,tcd->trd', edge_tiles.astype(jnp.bfloat16), picked, prefe...]
    scatter-add x1 -> x0, other arithmetic: 7.25 us -> none  [body(): jax.ops.segment_sum(received, local_index, num_segments=group_count * owned)]
  transfers between devices with their start and end apart: 3 -> 0, of which waited for: 2 -> 0; matrix products, arithmetic and copies ran while one was open for 3% -> 0% of each run, Pallas kernels for 0% -> 0%
where the time goes in v1:
time: 92.4 us; the launch traced here: 92.1 us
  Pallas kernels  84.6 us (92%)
  local copies, waits for them, and re-layouts  6.02 us (7%)
    pallas_call x1, Pallas kernels, body(): pl.pallas_call(functools.partial(exchange_kernel, n_grp, n_mem), out_shap...  81.9 us
    unnamed x20, local copies, waits for them, and re-layouts  5.94 us
    pallas_call x1, Pallas kernels, body(): pl.pallas_call(local_kernel, out_shape=jax.ShapeDtypeStruct((HALVES, slot...  2.63 us

profile of v1, /device:TPU:1, one launch (start us, length us, event | category | flops | bytes accessed | tf_op | source)
XLA Modules:
  0.0 92.1 jit_solution(16965393609028755692)
XLA Ops:
  0.6 0.0 copy-start.8
  0.6 0.0 copy-start.4
  0.7 0.7 fusion.3
  1.4 0.1 reshape.14
  1.4 0.1 add_bitcast_fusion
  1.5 0.0 copy-start
  1.5 1.6 %copy-done = s32[32,128,128]{2,1,0:T(8,128)S(1)} copy-done((s32[32,128,128]{2,1,0:T(8,128)S(1)}, s32[32,128,128]{2,1,0:T(8,128)}, u32[]{:S(2)}) %copy-start) | copy-done | bytes 2097176
  3.1 0.0 copy-start.1
  3.1 0.9 %copy-done.1 = bf16[512,256]{1,0:T(8,128)(2,1)S(1)} copy-done((bf16[512,256]{1,0:T(8,128)(2,1)S(1)}, bf16[512,256]{1,0:T(8,128)(2,1)}, u32[]{:S(2)}) %copy-start.1) | copy-done | bytes 262168
  4.1 0.0 copy-start.5
  4.1 0.7 copy-done.5
  4.8 0.0 copy-start.6
  4.8 0.7 copy-done.6
  5.4 0.0 copy-start.7
  5.4 0.7 copy-done.7
  6.1 0.0 copy-start.2
  6.1 0.0 copy-start.3
  6.1 2.6 %local_sums.1.part = bf16[2,1024,128]{2,1,0:T(8,128)(2,1)S(1)} custom-call(s32[32]{0:T(128)S(1)} %copy-done.6, s32[32]{0:T(128)S(1)} %copy-done.7, bf16[512,256]{1,0:T(8,128)(2,1)S(1)} %copy-done.1, s32[4,128]{1,0:T(4,128)S(1)} %bitcast.4, s32[32,128,128]{2,1,0:T(8,128)S(1)} %copy-done), custom_call_target="tpu_custom_call" | custom-call | tf_op jit(solution)/shard_map/local_sums/pallas_call | solution.py:243
  8.7 0.0 copy-done.8
  8.7 0.0 copy-done.4
  8.7 0.0 copy-done.2
  8.7 0.0 copy-done.3
  8.7 81.9 %exchange.1 = (bf16[32,256]{1,0:T(8,128)(2,1)S(1)}, bf16[1024,256]{1,0:T(8,128)(2,1)S(1)}) custom-call(bf16[2,1024,128]{2,1,0:T(8,128)(2,1)S(1)} %local_sums.1.part, s32[16,8,128]{2,1,0:T(8,128)S(1)} %broadcast_in_dim.8.ids, bf16[32,256]{1,0:T(8,128)(2,1)S(1)} %copy-done.4, s32[1,32]{1,0:T(1,128)S(1)} %bitcast.5, bf16[256,256]{1,0:T(8,128)(2,1)S(1)} %copy-done.2, ...), custom_call_target="tpu_custom_call" | custom-call | tf_op jit(solution)/shard_map/exchange/pallas_call | solution.py:259
  90.7 0.6 copy.14
  91.3 0.8 copy.15
  (1 shorter events, 0.0 us)
Async XLA Ops:
  0.6 8.1 %copy-start.8 = (s32[32]{0:T(128)S(1)}, s32[32]{0:T(128)}, u32[]{:S(2)}) copy-start(s32[32]{0:T(128)} %param.17) | copy-start | bytes 388
  0.6 8.1 %copy-start.4 = (bf16[32,256]{1,0:T(8,128)(2,1)S(1)}, bf16[32,256]{1,0:T(8,128)(2,1)}, u32[]{:S(2)}) copy-start(bf16[32,256]{1,0:T(8,128)(2,1)} %mrow.1) | copy-start | bytes 49156
  1.5 1.6 %copy-start = (s32[32,128,128]{2,1,0:T(8,128)S(1)}, s32[32,128,128]{2,1,0:T(8,128)}, u32[]{:S(2)}) copy-start(s32[32,128,128]{2,1,0:T(8,128)} %tiles.1) | copy-start | bytes 6291460
  3.1 0.9 %copy-start.1 = (bf16[512,256]{1,0:T(8,128)(2,1)S(1)}, bf16[512,256]{1,0:T(8,128)(2,1)}, u32[]{:S(2)}) copy-start(bf16[512,256]{1,0:T(8,128)(2,1)} %src.1) | copy-start | bytes 786436
  4.1 0.7 copy-start.5
  4.8 0.7 copy-start.6
  5.4 0.7 copy-start.7
  6.1 2.7 %copy-start.2 = (bf16[256,256]{1,0:T(8,128)(2,1)S(1)}, bf16[256,256]{1,0:T(8,128)(2,1)}, u32[]{:S(2)}) copy-start(bf16[256,256]{1,0:T(8,128)(2,1)} %w1.1) | copy-start | bytes 393220
  6.1 2.7 %copy-start.3 = (bf16[256,256]{1,0:T(8,128)(2,1)S(1)}, bf16[256,256]{1,0:T(8,128)(2,1)}, u32[]{:S(2)}) copy-start(bf16[256,256]{1,0:T(8,128)(2,1)} %w2.1) | copy-start | bytes 393220

commit v2 on v0

v2 whole, which is shorter than its diff:
```python
import functools

import jax
import jax.numpy as jnp
from jax import lax
from jax.experimental import pallas as pl
from jax.experimental.pallas import tpu as pltpu
from jax.sharding import PartitionSpec as P

MESH = pl.DeviceIdType.MESH
NX = 4
NC = 2
LANE = 128
HALVES = 2
PARTS = 3
FETCH = 4


def log2(n):
    assert n & (n - 1) == 0
    return n.bit_length() - 1


def kernel(
    n_grp, n_mem, trow_h, tcol_h, src_h, deg_h, tiles_h, ids_h, mrow_h, mdeg_h, w1_h, w2_h, newm, mirror,
    trow, tcol, src, deg, tiles, idin, mrow, mdeg, w1, w2,
    scaled, bits, lhs, rhs, part, place, idrecv, even, odd, put, take, precv, col, xacc, xrecv, zsend, zrecv, table, served,
    newv, out_s, in_s, tile_s, id_s, id_r, y_s, y_r, x_s, x_r, z_s, z_r, gz_s, gz_r, gx_s, gx_r, b_s, b_r,
):
    g = lax.axis_index("grp")
    m = lax.axis_index("mem")
    n_z, n_y = n_grp // NX, n_mem // NC
    x, z = lax.rem(g, NX), g // NX
    c, y = lax.rem(m, NC), m // NC
    tile = tiles.shape[1]
    n_tiles = tiles.shape[0]
    slot_total = precv.shape[1]
    slots = slot_total // n_mem
    owned = mrow.shape[0]
    half_z = n_z // 2
    z_part = n_z // PARTS
    rows = z_part * owned

    def mem_of(dy, dc):
        return lax.rem(y + dy + n_y, n_y) * NC + lax.rem(c + dc, NC)

    def grp_x(j):
        return z * NX + lax.rem(x + j + NX, NX)

    def grp_z(k):
        return lax.rem(z + k + n_z, n_z) * NX + x

    def pos(k):
        return 2 * abs(k - half_z) - (1 if k < half_z else 0)

    y_order = [0] + [s for d in range(1, n_y // 2) for s in (n_y - d, d)] + [n_y // 2]
    mem_order = [(dy, dc) for dy in reversed(y_order) for dc in range(NC) if (dy, dc) != (0, 0)]
    x_order = sorted(range(1, NX), key=lambda j: -min(j, NX - j))
    z_order = sorted(range(1, n_z), key=pos)

    fetch = [
        pltpu.make_async_copy(a, b, in_s.at[i])
        for i, (a, b) in enumerate([
            (deg_h, deg), (src_h, src), (trow_h, trow), (tcol_h, tcol), (ids_h, idin),
            (mrow_h, mrow), (mdeg_h, mdeg), (w1_h, w1), (w2_h, w2)])
    ]
    step = n_tiles // FETCH
    fetch_tiles = [
        pltpu.make_async_copy(tiles_h.at[pl.ds(i * step, step)], tiles.at[pl.ds(i * step, step)], tile_s.at[i])
        for i in range(FETCH)
    ]
    for copy in fetch[:5]:
        copy.start()
    for copy in fetch_tiles:
        copy.start()
    for copy in fetch[5:]:
        copy.start()

    barrier = pltpu.get_barrier_semaphore()
    partners = [(grp_z(k), m) for k in z_order] + [(g, mem_of(*d)) for d in mem_order] + [
        (grp_x(j), m) for j in x_order]
    for who in partners:
        pl.semaphore_signal(barrier, inc=1, device_id=who, device_id_type=MESH)

    fetch[0].wait()
    fetch[1].wait()
    scale = lax.rsqrt(deg[...].astype(jnp.float32))
    for k in range(src.shape[0] // tile):
        column = jnp.broadcast_to(scale[k : k + 1, :], (tile, tile)).T
        for h in range(HALVES):
            at = (pl.ds(k * tile, tile), pl.ds(h * LANE, LANE))
            scaled[h, k] = (src[at].astype(jnp.float32) * column).astype(jnp.bfloat16)
    for copy in fetch[2:5]:
        copy.wait()

    ids = idin[...]
    group = jnp.right_shift(ids, log2(owned * n_mem))
    dx = jnp.bitwise_and(group, NX - 1) - x
    dx = jnp.where(dx < 0, dx + NX, dx)
    dz = jnp.right_shift(group, log2(NX)) - z
    dz = jnp.where(dz < 0, dz + n_z, dz)
    order = 2 * jnp.abs(dz - half_z) - jnp.where(dz < half_z, 1, 0)
    z_group = jnp.right_shift(order, log2(z_part))
    spots = (z_group * NX + dx) * rows + jnp.bitwise_and(order, z_part - 1) * owned + jnp.bitwise_and(
        ids, owned - 1)

    for k in range(n_y):
        place[k] = spots[k : k + 1, :]

    for i in range(FETCH):
        fetch_tiles[i].wait()
        for t in range(i * step, (i + 1) * step):
            bits[t] = tiles[t].astype(jnp.float32).astype(jnp.bfloat16)

    def sums_for(h, dy):
        block = lax.rem(y + dy, n_y)
        if h == 0:
            for t in range(n_tiles):
                edges = bits[t]
                lhs[dy, :, t * tile : (t + 1) * tile] = jnp.where(trow[t] == block, edges, jnp.zeros_like(edges))
        part[h, dy] = jnp.dot(lhs[dy], rhs[h], preferred_element_type=jnp.float32).astype(jnp.bfloat16)


    def slot_of(dy, dc):
        return dy * NC + dc

    def id_copy(dy, dc):
        return pltpu.make_async_remote_copy(
            src_ref=place.at[lax.rem(y + dy, n_y)], dst_ref=idrecv.at[slot_of(dy, dc)], send_sem=id_s, recv_sem=id_r,
            device_id=(g, mem_of(dy, dc)), device_id_type=MESH)

    def y_copy(h, dy, dc):
        to = mem_of(dy, dc)
        return pltpu.make_async_remote_copy(
            src_ref=part.at[h, dy, pl.ds(pl.multiple_of(lax.rem(to, NC) * slots, slots), slots)],
            dst_ref=precv.at[h, pl.ds(slot_of(dy, dc) * slots, slots)],
            send_sem=y_s.at[h], recv_sem=y_r.at[h], device_id=(g, to), device_id_type=MESH)

    def x_copy(h, q, j):
        return pltpu.make_async_remote_copy(
            src_ref=col.at[h, q, j], dst_ref=xrecv.at[h, q, j], send_sem=x_s.at[h], recv_sem=x_r.at[h, q],
            device_id=(grp_x(j), m), device_id_type=MESH)

    def z_copy(h, k):
        return pltpu.make_async_remote_copy(
            src_ref=zsend.at[h, pos(k)], dst_ref=zrecv.at[h, k], send_sem=z_s.at[h], recv_sem=z_r.at[h],
            device_id=(grp_z(k), m), device_id_type=MESH)

    def z_rows(k):
        return pos(k) // z_part, pl.ds(pos(k) % z_part * owned, owned)

    def gz_copy(h, k):
        q, at = z_rows(0)
        to_q, to_at = z_rows((n_z - k) % n_z)
        return pltpu.make_async_remote_copy(
            src_ref=table.at[h, q, 0, at], dst_ref=table.at[h, to_q, 0, to_at], send_sem=gz_s,
            recv_sem=gz_r.at[h, to_q], device_id=(grp_z(k), m), device_id_type=MESH)

    def gx_copy(h, q, j):
        return pltpu.make_async_remote_copy(
            src_ref=table.at[h, q, 0], dst_ref=table.at[h, q, NX - j], send_sem=gx_s.at[h], recv_sem=gx_r.at[h],
            device_id=(grp_x(j), m), device_id_type=MESH)

    def b_copy(h, dy, dc):
        to = mem_of(-dy, dc)
        return pltpu.make_async_remote_copy(
            src_ref=served.at[h, pl.ds(slot_of(dy, dc) * slots, slots)],
            dst_ref=mirror.at[pl.ds(pl.multiple_of(m * slots, slots), slots), pl.ds(h * LANE, LANE)],
            send_sem=b_s.at[h], recv_sem=b_r.at[h], device_id=(g, to), device_id_type=MESH)

    def drain(ref, sem):
        pltpu.make_async_copy(ref, ref, sem).wait()

    mine = pl.ds(pl.multiple_of(m * slots, slots), slots)
    idrecv[0] = place[y]
    for h in range(HALVES):
        for t in range(n_tiles):
            rhs[h, t * tile : (t + 1) * tile, :] = scaled[h, tcol[t]]
        for i, dy in enumerate(reversed(y_order)):
            sums_for(h, dy)
            if h == 0 and i == 0:
                pl.semaphore_wait(barrier, len(partners))
                for d in mem_order:
                    id_copy(*d).start()
            for dc in range(NC):
                if (dy, dc) != (0, 0):
                    y_copy(h, dy, dc).start()
        precv[h, 0:slots] = part[h, 0, pl.ds(pl.multiple_of(c * slots, slots), slots), :]

    drain(idrecv.at[pl.ds(1, n_mem - 1)], id_r)
    for k in range(n_y):
        even[k : k + 1, :] = idrecv[NC * k]
        odd[k : k + 1, :] = idrecv[NC * k + 1]
    lane = lax.broadcasted_iota(jnp.int32, (n_y, LANE), 1)
    low = jnp.where(c == 0, even[...], pltpu.roll(even[...], slots, 1))
    high = jnp.where(c == 0, pltpu.roll(odd[...], slots, 1), odd[...])
    spot = jnp.where(lane < slots, low, high)
    n_table = PARTS * NX * rows
    even[...] = spot

    def build_put(v, carry):
        row = lax.broadcasted_iota(jnp.int32, (LANE, LANE), 0) + v * LANE
        for k in range(n_y):
            put[pl.ds(pl.multiple_of(v * LANE, LANE), LANE), k * LANE : (k + 1) * LANE] = jnp.where(
                row == even[k : k + 1, :], 1.0, 0.0).astype(jnp.bfloat16)
        return carry

    lax.fori_loop(0, n_table // LANE, build_put, 0)

    group_rows = NX * rows
    for h in range(HALVES):
        drain(precv.at[h, pl.ds(slots, slot_total - slots)], y_r.at[h])
        for q in range(PARTS):
            block = jnp.dot(put[q * group_rows : (q + 1) * group_rows, :], precv[h], preferred_element_type=jnp.float32)
            for j in x_order:
                col[h, q, j] = block[j * rows : (j + 1) * rows].astype(jnp.bfloat16)
                x_copy(h, q, j).start()
            xacc[h, q] = block[0:rows]

    for h in range(HALVES):
        for q in range(PARTS):
            drain(xrecv.at[h, q, pl.ds(1, NX - 1)], x_r.at[h, q])
            total = xacc[h, q]
            for j in range(1, NX):
                total = total + xrecv[h, q, j].astype(jnp.float32)
            xacc[h, q] = total
            for i in range(z_part):
                zsend[h, q * z_part + i] = total[i * owned : (i + 1) * owned].astype(jnp.bfloat16)
            for k in z_order:
                if pos(k) // z_part == q:
                    z_copy(h, k).start()

    def build_take(k, carry):
        column = jnp.broadcast_to(even[pl.ds(k, 1), :], (LANE, LANE)).T
        for v in range(n_table // LANE):
            row = lax.broadcasted_iota(jnp.int32, (LANE, LANE), 1) + v * LANE
            take[pl.ds(pl.multiple_of(k * LANE, LANE), LANE), v * LANE : (v + 1) * LANE] = jnp.where(
                column == row, 1.0, 0.0).astype(jnp.bfloat16)
        return carry

    lax.fori_loop(0, n_y, build_take, 0)
    for copy in fetch[5:]:
        copy.wait()
    drain(idrecv.at[pl.ds(1, n_mem - 1)], id_s)
    for h in range(HALVES):
        drain(precv.at[h, pl.ds(slots, slot_total - slots)], y_s.at[h])
        drain(xrecv.at[h, :, pl.ds(1, NX - 1)], x_s.at[h])

    own_q, own_at = z_rows(0)
    sums = []
    for h in range(HALVES):
        drain(zrecv.at[h, pl.ds(1, n_z - 1)], z_r.at[h])
        total = xacc[h, own_q, own_at, :]
        for k in range(1, n_z):
            total = total + zrecv[h, k].astype(jnp.float32)
        sums.append(total)

    scale = lax.rsqrt(mdeg[...].astype(jnp.float32))
    diagonal = lax.broadcasted_iota(jnp.int32, (owned, owned), 0) == lax.broadcasted_iota(
        jnp.int32, (owned, owned), 1)
    scale = jnp.sum(jnp.where(diagonal, jnp.broadcast_to(scale, (owned, owned)), 0.0), axis=1, keepdims=True)
    neigh = jnp.concatenate(sums, axis=1) * scale
    embed = mrow[...].astype(jnp.float32)
    first = (embed + neigh).astype(jnp.bfloat16)
    second = (neigh * embed).astype(jnp.bfloat16)
    result = jnp.dot(first, w1[...], preferred_element_type=jnp.float32) + jnp.dot(
        second, w2[...], preferred_element_type=jnp.float32)
    new = jnp.where(result > 0, result, 0.2 * result).astype(jnp.bfloat16)
    for h in range(HALVES):
        table[h, own_q, 0, own_at, :] = new[:, h * LANE : (h + 1) * LANE]

    for h in range(HALVES):
        for k in reversed(z_order):
            gz_copy(h, k).start()
    newv[...] = new
    keep = [pltpu.make_async_copy(newv, newm, out_s.at[0])]
    keep[0].start()
    for h, q in ((0, 2), (0, 1), (1, 2), (0, 0), (1, 1), (1, 0)):
        n_here = z_part - (1 if q == own_q else 0)
        drain(table.at[h, q, 0, pl.ds(0, n_here * owned)], gz_r.at[h, q])
        for j in x_order:
            gx_copy(h, q, j).start()

    for h in range(HALVES):
        drain(table.at[h, :, pl.ds(1, NX - 1)], gx_r.at[h])
        for first in (4, 2, 6, 0):
            at = slice(first * LANE, (first + 2) * LANE)
            served[h, at, :] = jnp.dot(
                take[at, :], table[h].reshape(n_table, LANE), preferred_element_type=jnp.float32
            ).astype(jnp.bfloat16)
            for d in mem_order:
                if d[0] // 2 * 2 == first:
                    b_copy(h, *d).start()
        keep.append(pltpu.make_async_copy(served.at[h, pl.ds(0, slots)], mirror.at[mine, pl.ds(h * LANE, LANE)], out_s.at[1 + h]))
        keep[-1].start()

    for copy in keep:
        copy.wait()

    drain(zrecv.at[:, pl.ds(1, n_z - 1)], gz_s)
    for h in range(HALVES):
        drain(zrecv.at[h, pl.ds(1, n_z - 1)], z_s.at[h])
        drain(table.at[h, :, pl.ds(1, NX - 1)], gx_s.at[h])
    for h in range(HALVES):
        drain(served.at[h, pl.ds(slots, slot_total - slots)], b_s.at[h])
        drain(served.at[h, pl.ds(slots, slot_total - slots)], b_r.at[h])


def hand_over(new_in, mirror_in, new_out, mirror_out, new_v, mirror_v, in_s, out_s):
    piece = mirror_v.shape[0] // (in_s.shape[0] - 1)
    views = [(new_in, new_v, new_out)] + [
        (mirror_in.at[at], mirror_v.at[at], mirror_out.at[at])
        for at in (pl.ds(i * piece, piece) for i in range(in_s.shape[0] - 1))]
    inward = [pltpu.make_async_copy(a, b, in_s.at[i]) for i, (a, b, _) in enumerate(views)]
    outward = [pltpu.make_async_copy(b, c, out_s.at[i]) for i, (_, b, c) in enumerate(views)]
    for copy in inward:
        copy.start()
    for first, then in zip(inward, outward):
        first.wait()
        then.start()
    for copy in outward:
        copy.wait()


def body(n_grp, n_mem, source_rows, source_degree, edge_tiles, tile_row, tile_col, mirror_ids,
         master_rows, master_degree, weight_one, weight_two):
    n_tiles, tile, _ = edge_tiles.shape
    src_dev, width = source_rows.shape
    slot_total = mirror_ids.shape[0]
    owned = master_rows.shape[0]
    n_z = n_grp // NX
    z_part = n_z // PARTS
    rows = z_part * owned
    n_table = n_z * NX * owned
    hbm = pl.BlockSpec(memory_space=pltpu.HBM)
    vmem = pl.BlockSpec(memory_space=pltpu.VMEM)
    bf, f32, i32 = jnp.bfloat16, jnp.float32, jnp.int32
    dma = pltpu.SemaphoreType.DMA
    operands = (
        tile_row, tile_col, source_rows, source_degree.reshape(-1, tile), edge_tiles, mirror_ids.reshape(-1, LANE),
        master_rows, master_degree.reshape(1, owned), weight_one, weight_two,
    )
    outs = pl.pallas_call(
        functools.partial(kernel, n_grp, n_mem),
        out_shape=(
            jax.ShapeDtypeStruct((owned, width), bf),
            jax.ShapeDtypeStruct((slot_total, width), bf),
        ),
        in_specs=[hbm] * len(operands),
        out_specs=(hbm, hbm),
        scratch_shapes=[
            pltpu.SMEM((n_tiles,), i32),
            pltpu.SMEM((n_tiles,), i32),
            pltpu.VMEM((src_dev, width), bf),
            pltpu.VMEM((src_dev // tile, tile), i32),
            pltpu.VMEM((n_tiles, tile, tile), i32),
            pltpu.VMEM((slot_total // LANE, LANE), i32),
            pltpu.VMEM((owned, width), bf),
            pltpu.VMEM((1, owned), i32),
            pltpu.VMEM((width, width), bf),
            pltpu.VMEM((width, width), bf),
            pltpu.VMEM((HALVES, src_dev // tile, tile, LANE), bf),
            pltpu.VMEM((n_tiles, tile, tile), bf),
            pltpu.VMEM((n_mem // NC, tile, n_tiles * tile), bf),
            pltpu.VMEM((HALVES, n_tiles * tile, LANE), bf),
            pltpu.VMEM((HALVES, n_mem // NC, tile, LANE), bf),
            pltpu.VMEM((n_mem // NC, 1, LANE), i32),
            pltpu.VMEM((n_mem, 1, LANE), i32),
            pltpu.VMEM((slot_total // LANE, LANE), i32),
            pltpu.VMEM((slot_total // LANE, LANE), i32),
            pltpu.VMEM((n_table, slot_total), bf),
            pltpu.VMEM((slot_total, n_table), bf),
            pltpu.VMEM((HALVES, slot_total, LANE), bf),
            pltpu.VMEM((HALVES, PARTS, NX, rows, LANE), bf),
            pltpu.VMEM((HALVES, PARTS, rows, LANE), f32),
            pltpu.VMEM((HALVES, PARTS, NX, rows, LANE), bf),
            pltpu.VMEM((HALVES, n_z, owned, LANE), bf),
            pltpu.VMEM((HALVES, n_z, owned, LANE), bf),
            pltpu.VMEM((HALVES, PARTS, NX, rows, LANE), bf),
            pltpu.VMEM((HALVES, slot_total, LANE), bf),
            pltpu.VMEM((owned, width), bf), dma((1 + HALVES,)),
            dma((len(operands) - 1,)), dma((FETCH,)),
            dma, dma,
            dma((HALVES,)), dma((HALVES,)),
            dma((HALVES,)), dma((HALVES, PARTS)),
            dma((HALVES,)), dma((HALVES,)),
            dma, dma((HALVES, PARTS)),
            dma((HALVES,)), dma((HALVES,)),
            dma((HALVES,)), dma((HALVES,)),
        ],
        compiler_params=pltpu.CompilerParams(
            collective_id=0, has_side_effects=True, vmem_limit_bytes=62 * 2**20),
        name="layer",
    )(*operands)
    return pl.pallas_call(
        hand_over,
        out_shape=tuple(jax.ShapeDtypeStruct(o.shape, o.dtype) for o in outs),
        in_specs=[hbm, hbm],
        out_specs=(hbm, hbm),
        scratch_shapes=[pltpu.VMEM(o.shape, o.dtype) for o in outs] + [dma((5,)), dma((5,))],
        compiler_params=pltpu.CompilerParams(vmem_limit_bytes=62 * 2**20),
        name="hand_over",
    )(*outs)


def solution(mesh):
    both = ("grp", "mem")
    in_specs = (
        P(both, None), P(both), P(both, None, None), P(both), P(both), P(both),
        P(both, None), P(both), P(), P(),
    )
    out_specs = (P(both, None), P(both, None))
    fn = functools.partial(body, mesh.shape["grp"], mesh.shape["mem"])
    return jax.shard_map(fn, mesh=mesh, in_specs=in_specs, out_specs=out_specs, check_vma=False)
```

time: 622 us -> 74.5 us (0.12)
  waiting for transfers between devices: 444 us -> 0 us
  blocking collectives: 107 us -> 0 us
  Pallas kernels: 0 us -> 73.5 us
  starting transfers between devices: 21.1 us -> 0 us
  local copies, waits for them, and re-layouts: 14.2 us -> 0 us
  between operations: 14.1 us -> 0.8 us
  other arithmetic: 10.4 us -> 0 us
  matrix products: 9.81 us -> 0 us
    reduce_scatter x1 -> x0, waiting for transfers between devices: 418 us -> none  [body(): shares = lax.psum_scatter(column, 'grp', scatter_dimension=0, tiled=True)]
    pallas_call x0 -> x2, Pallas kernels: none -> 73.5 us  [the longest x1 71.6 us: body(): pl.pallas_call(functools.partial(kernel, n_grp, n_mem), out_shape=(jax.Sh...]
    all_gather x1 -> x0, blocking collectives: 56.1 us -> none  [body(): column_new = lax.all_gather(new_master, 'grp', axis=0, tiled=True)]
    all_to_all x1 -> x0, blocking collectives: 50.6 us -> none  [body(): lax.all_to_all(served, 'mem', split_axis=0, concat_axis=0, tiled=True)]
    all_to_all x2 -> x0, waiting for transfers between devices: 26.5 us -> none  [the longest x1 26.5 us: body(): lax.all_to_all(partial_value, 'mem', split_axis=0, concat_axis=0, tiled=T...]
    all_to_all x2 -> x0, starting transfers between devices: 21 us -> none  [the longest x1 13.8 us: body(): lax.all_to_all(mirror_ids, 'mem', split_axis=0, concat_axis=0, tiled=True)]
    dot_general x4 -> x0, matrix products: 9.81 us -> none  [the longest x1 4.28 us: body(): jnp.einsum('trc,tcd->trd', edge_tiles.astype(jnp.bfloat16), picked, prefe...]
    scatter-add x1 -> x0, other arithmetic: 7.25 us -> none  [body(): jax.ops.segment_sum(received, local_index, num_segments=group_count * owned)]
  transfers between devices with their start and end apart: 3 -> 0, of which waited for: 2 -> 0; matrix products, arithmetic and copies ran while one was open for 3% -> 0% of each run, Pallas kernels for 0% -> 0%
where the time goes in v2:
time: 74.5 us; the launch traced here: 74.3 us
  Pallas kernels  73.5 us (99%)
  between operations  0.8 us (1%)
    pallas_call x1, Pallas kernels, body(): pl.pallas_call(functools.partial(kernel, n_grp, n_mem), out_shape=(jax.Sh...  71.6 us
    pallas_call x1, Pallas kernels, body(): pl.pallas_call(hand_over, out_shape=tuple((jax.ShapeDtypeStruct(o.shape,...  1.85 us

profile of v2, /device:TPU:1, one launch (start us, length us, event | category | flops | bytes accessed | tf_op | source)
XLA Modules:
  0.0 74.3 jit_solution(13798924008250130445)
XLA Ops:
  0.6 71.6 %layer.1 = (bf16[32,256]{1,0:T(8,128)(2,1)}, bf16[1024,256]{1,0:T(8,128)(2,1)}) custom-call(s32[32]{0:T(128)} %trow_h.1, s32[32]{0:T(128)} %tcol_h.1, bf16[512,256]{1,0:T(8,128)(2,1)} %src_h.1, s32[4,128]{1,0:T(4,128)} %bitcast.4, s32[32,128,128]{2,1,0:T(8,128)} %tiles_h.1, s32[8,128]{1,0:T(8,128)} %bitcast.3, bf16[32,256]{1,0:T(8,128)(2,1)} %mrow_h.1, ...), custom_call_target="tpu_custom_call" | custom-call | tf_op jit(solution)/shard_map/layer/pallas_call | solution.py:343
  72.3 1.9 %hand_over.1 = (bf16[32,256]{1,0:T(8,128)(2,1)}, bf16[1024,256]{1,0:T(8,128)(2,1)}) custom-call(bf16[32,256]{1,0:T(8,128)(2,1)} %get-tuple-element.4.new_in, bf16[1024,256]{1,0:T(8,128)(2,1)} %get-tuple-element.5.mirror_in), custom_call_target="tpu_custom_call" | custom-call | tf_op jit(solution)/shard_map/hand_over/pallas_call | solution.py:395

commit v3 on v2

--- a/solution.py
+++ b/solution.py
@@ -12,7 +12,7 @@
 NC = 2
 LANE = 128
 HALVES = 2
-PARTS = 3
+PARTS = 6
 FETCH = 4
 
 
@@ -269,17 +269,20 @@
     for h in range(HALVES):
         table[h, own_q, 0, own_at, :] = new[:, h * LANE : (h + 1) * LANE]
 
-    for h in range(HALVES):
-        for k in reversed(z_order):
-            gz_copy(h, k).start()
+    for k in reversed(z_order):
+        gz_copy(0, k).start()
     newv[...] = new
     keep = [pltpu.make_async_copy(newv, newm, out_s.at[0])]
     keep[0].start()
-    for h, q in ((0, 2), (0, 1), (1, 2), (0, 0), (1, 1), (1, 0)):
-        n_here = z_part - (1 if q == own_q else 0)
-        drain(table.at[h, q, 0, pl.ds(0, n_here * owned)], gz_r.at[h, q])
-        for j in x_order:
-            gx_copy(h, q, j).start()
+    for h in range(HALVES):
+        for q in reversed(range(PARTS)):
+            n_here = z_part - (1 if q == own_q else 0)
+            drain(table.at[h, q, 0, pl.ds(0, n_here * owned)], gz_r.at[h, q])
+            for j in x_order:
+                gx_copy(h, q, j).start()
+            if (h, q) == (0, PARTS // 2):
+                for k in reversed(z_order):
+                    gz_copy(1, k).start()
 
     for h in range(HALVES):
         drain(table.at[h, :, pl.ds(1, NX - 1)], gx_r.at[h])

time: 74.5 us -> 72.5 us (0.973)
  Pallas kernels: 73.5 us -> 71.5 us
    pallas_call x1, Pallas kernels: 71.6 us -> 69.7 us  [body(): pl.pallas_call(functools.partial(kernel, n_grp, n_mem), out_shape=(jax.Sh...]
where the time goes in v3:
time: 72.5 us; the launch traced here: 72.3 us
  Pallas kernels  71.5 us (99%)
  between operations  0.8 us (1%)
    pallas_call x1, Pallas kernels, body(): pl.pallas_call(functools.partial(kernel, n_grp, n_mem), out_shape=(jax.Sh...  69.7 us
    pallas_call x1, Pallas kernels, body(): pl.pallas_call(hand_over, out_shape=tuple((jax.ShapeDtypeStruct(o.shape,...  1.85 us

profile of v3, /device:TPU:1, one launch (start us, length us, event | category | flops | bytes accessed | tf_op | source)
XLA Modules:
  0.0 72.3 jit_solution(6261847018486379750)
XLA Ops:
  0.6 69.7 %layer.1 = (bf16[32,256]{1,0:T(8,128)(2,1)}, bf16[1024,256]{1,0:T(8,128)(2,1)}) custom-call(s32[32]{0:T(128)} %trow_h.1, s32[32]{0:T(128)} %tcol_h.1, bf16[512,256]{1,0:T(8,128)(2,1)} %src_h.1, s32[4,128]{1,0:T(4,128)} %bitcast.4, s32[32,128,128]{2,1,0:T(8,128)} %tiles_h.1, s32[8,128]{1,0:T(8,128)} %bitcast.3, bf16[32,256]{1,0:T(8,128)(2,1)} %mrow_h.1, ...), custom_call_target="tpu_custom_call" | custom-call | tf_op jit(solution)/shard_map/layer/pallas_call | solution.py:346
  70.3 1.9 %hand_over.1 = (bf16[32,256]{1,0:T(8,128)(2,1)}, bf16[1024,256]{1,0:T(8,128)(2,1)}) custom-call(bf16[32,256]{1,0:T(8,128)(2,1)} %get-tuple-element.4.new_in, bf16[1024,256]{1,0:T(8,128)(2,1)} %get-tuple-element.5.mirror_in), custom_call_target="tpu_custom_call" | custom-call | tf_op jit(solution)/shard_map/hand_over/pallas_call | solution.py:398

commit v4 on v3

--- a/solution.py
+++ b/solution.py
@@ -25,7 +25,7 @@
     n_grp, n_mem, trow_h, tcol_h, src_h, deg_h, tiles_h, ids_h, mrow_h, mdeg_h, w1_h, w2_h, newm, mirror,
     trow, tcol, src, deg, tiles, idin, mrow, mdeg, w1, w2,
     scaled, bits, lhs, rhs, part, place, idrecv, even, odd, put, take, precv, col, xacc, xrecv, zsend, zrecv, table, served,
-    newv, out_s, in_s, tile_s, id_s, id_r, y_s, y_r, x_s, x_r, z_s, z_r, gz_s, gz_r, gx_s, gx_r, b_s, b_r,
+    newv, out_s, up_s, down_s, in_s, tile_s, id_s, id_r, y_s, y_r, x_s, x_r, z_s, z_r, gz_s, gz_r, gx_s, gx_r, b_s, b_r,
 ):
     g = lax.axis_index("grp")
     m = lax.axis_index("mem")
@@ -77,8 +77,8 @@
         copy.start()
 
     barrier = pltpu.get_barrier_semaphore()
-    partners = [(grp_z(k), m) for k in z_order] + [(g, mem_of(*d)) for d in mem_order] + [
-        (grp_x(j), m) for j in x_order]
+    partners = [(g, mem_of(*d)) for d in mem_order] + [(grp_x(j), m) for j in x_order] + [
+        (grp_z(k), m) for k in (1, n_z - 1)]
     for who in partners:
         pl.semaphore_signal(barrier, inc=1, device_id=who, device_id_type=MESH)
 
@@ -107,6 +107,11 @@
     for k in range(n_y):
         place[k] = spots[k : k + 1, :]
 
+    def fill_rhs(h):
+        for t in range(n_tiles):
+            rhs[h, t * tile : (t + 1) * tile, :] = scaled[h, tcol[t]]
+
+    fill_rhs(0)
     for i in range(FETCH):
         fetch_tiles[i].wait()
         for t in range(i * step, (i + 1) * step):
@@ -168,25 +173,39 @@
             dst_ref=mirror.at[pl.ds(pl.multiple_of(m * slots, slots), slots), pl.ds(h * LANE, LANE)],
             send_sem=b_s.at[h], recv_sem=b_r.at[h], device_id=(g, to), device_id_type=MESH)
 
+    def tell(r):
+        if r < half_z - 1:
+            pl.semaphore_signal(up_s.at[r], inc=1, device_id=(grp_z(1), m), device_id_type=MESH)
+            pl.semaphore_signal(down_s.at[r], inc=1, device_id=(grp_z(n_z - 1), m), device_id_type=MESH)
+
+    def hear(r):
+        pl.semaphore_wait(up_s.at[r], 1)
+        pl.semaphore_wait(down_s.at[r], 1)
+        tell(r + 1)
+
     def drain(ref, sem):
         pltpu.make_async_copy(ref, ref, sem).wait()
 
     mine = pl.ds(pl.multiple_of(m * slots, slots), slots)
     idrecv[0] = place[y]
     for h in range(HALVES):
-        for t in range(n_tiles):
-            rhs[h, t * tile : (t + 1) * tile, :] = scaled[h, tcol[t]]
+        if h:
+            fill_rhs(h)
         for i, dy in enumerate(reversed(y_order)):
             sums_for(h, dy)
             if h == 0 and i == 0:
                 pl.semaphore_wait(barrier, len(partners))
-                for d in mem_order:
-                    id_copy(*d).start()
             for dc in range(NC):
                 if (dy, dc) != (0, 0):
                     y_copy(h, dy, dc).start()
+            if h == 0 and i == 0:
+                tell(0)
+            if h == 0 and i == 2:
+                for d in mem_order:
+                    id_copy(*d).start()
         precv[h, 0:slots] = part[h, 0, pl.ds(pl.multiple_of(c * slots, slots), slots), :]
 
+    hear(0)
     drain(idrecv.at[pl.ds(1, n_mem - 1)], id_r)
     for k in range(n_y):
         even[k : k + 1, :] = idrecv[NC * k]
@@ -207,6 +226,8 @@
 
     lax.fori_loop(0, n_table // LANE, build_put, 0)
 
+    hear(1)
+
     group_rows = NX * rows
     for h in range(HALVES):
         drain(precv.at[h, pl.ds(slots, slot_total - slots)], y_r.at[h])
@@ -216,6 +237,9 @@
                 col[h, q, j] = block[j * rows : (j + 1) * rows].astype(jnp.bfloat16)
                 x_copy(h, q, j).start()
             xacc[h, q] = block[0:rows]
+        if h == 0:
+            for r in range(2, half_z - 1):
+                hear(r)
 
     for h in range(HALVES):
         for q in range(PARTS):
@@ -382,6 +406,7 @@
             pltpu.VMEM((HALVES, PARTS, NX, rows, LANE), bf),
             pltpu.VMEM((HALVES, slot_total, LANE), bf),
             pltpu.VMEM((owned, width), bf), dma((1 + HALVES,)),
+            pltpu.SemaphoreType.REGULAR((n_z // 2 - 1,)), pltpu.SemaphoreType.REGULAR((n_z // 2 - 1,)),
             dma((len(operands) - 1,)), dma((FETCH,)),
             dma, dma,
             dma((HALVES,)), dma((HALVES,)),

time: 72.5 us -> 71.5 us (0.986)
  Pallas kernels: 71.5 us -> 70.4 us
    pallas_call x1, Pallas kernels: 69.7 us -> 68.6 us  [body(): pl.pallas_call(functools.partial(kernel, n_grp, n_mem), out_shape=(jax.Sh...]
where the time goes in v4:
time: 71.5 us; the launch traced here: 71.2 us
  Pallas kernels  70.4 us (98%)
  between operations  0.8 us (1%)
    pallas_call x1, Pallas kernels, body(): pl.pallas_call(functools.partial(kernel, n_grp, n_mem), out_shape=(jax.Sh...  68.6 us
    pallas_call x1, Pallas kernels, body(): pl.pallas_call(hand_over, out_shape=tuple((jax.ShapeDtypeStruct(o.shape,...  1.85 us

profile of v4, /device:TPU:1, one launch (start us, length us, event | category | flops | bytes accessed | tf_op | source)
XLA Modules:
  0.0 71.2 jit_solution(4927586067964849468)
XLA Ops:
  0.6 68.6 %layer.1 = (bf16[32,256]{1,0:T(8,128)(2,1)}, bf16[1024,256]{1,0:T(8,128)(2,1)}) custom-call(s32[32]{0:T(128)} %trow_h.1, s32[32]{0:T(128)} %tcol_h.1, bf16[512,256]{1,0:T(8,128)(2,1)} %src_h.1, s32[4,128]{1,0:T(4,128)} %bitcast.4, s32[32,128,128]{2,1,0:T(8,128)} %tiles_h.1, s32[8,128]{1,0:T(8,128)} %bitcast.3, bf16[32,256]{1,0:T(8,128)(2,1)} %mrow_h.1, ...), custom_call_target="tpu_custom_call" | custom-call | tf_op jit(solution)/shard_map/layer/pallas_call | solution.py:370
  69.2 1.9 %hand_over.1 = (bf16[32,256]{1,0:T(8,128)(2,1)}, bf16[1024,256]{1,0:T(8,128)(2,1)}) custom-call(bf16[32,256]{1,0:T(8,128)(2,1)} %get-tuple-element.4.new_in, bf16[1024,256]{1,0:T(8,128)(2,1)} %get-tuple-element.5.mirror_in), custom_call_target="tpu_custom_call" | custom-call | tf_op jit(solution)/shard_map/hand_over/pallas_call | solution.py:423

commit v5 on v4

--- a/solution.py
+++ b/solution.py
@@ -25,7 +25,7 @@
     n_grp, n_mem, trow_h, tcol_h, src_h, deg_h, tiles_h, ids_h, mrow_h, mdeg_h, w1_h, w2_h, newm, mirror,
     trow, tcol, src, deg, tiles, idin, mrow, mdeg, w1, w2,
     scaled, bits, lhs, rhs, part, place, idrecv, even, odd, put, take, precv, col, xacc, xrecv, zsend, zrecv, table, served,
-    newv, out_s, up_s, down_s, in_s, tile_s, id_s, id_r, y_s, y_r, x_s, x_r, z_s, z_r, gz_s, gz_r, gx_s, gx_r, b_s, b_r,
+    up_s, down_s, in_s, tile_s, id_s, id_r, y_s, y_r, x_s, x_r, z_s, z_r, gz_s, gz_r, gx_s, gx_r, b_s, b_r,
 ):
     g = lax.axis_index("grp")
     m = lax.axis_index("mem")
@@ -295,9 +295,7 @@
 
     for k in reversed(z_order):
         gz_copy(0, k).start()
-    newv[...] = new
-    keep = [pltpu.make_async_copy(newv, newm, out_s.at[0])]
-    keep[0].start()
+    newm[...] = new
     for h in range(HALVES):
         for q in reversed(range(PARTS)):
             n_here = z_part - (1 if q == own_q else 0)
@@ -318,11 +316,7 @@
             for d in mem_order:
                 if d[0] // 2 * 2 == first:
                     b_copy(h, *d).start()
-        keep.append(pltpu.make_async_copy(served.at[h, pl.ds(0, slots)], mirror.at[mine, pl.ds(h * LANE, LANE)], out_s.at[1 + h]))
-        keep[-1].start()
-
-    for copy in keep:
-        copy.wait()
+        mirror[mine, h * LANE : (h + 1) * LANE] = served[h, 0:slots, :]
 
     drain(zrecv.at[:, pl.ds(1, n_z - 1)], gz_s)
     for h in range(HALVES):
@@ -333,19 +327,14 @@
         drain(served.at[h, pl.ds(slots, slot_total - slots)], b_r.at[h])
 
 
-def hand_over(new_in, mirror_in, new_out, mirror_out, new_v, mirror_v, in_s, out_s):
-    piece = mirror_v.shape[0] // (in_s.shape[0] - 1)
-    views = [(new_in, new_v, new_out)] + [
-        (mirror_in.at[at], mirror_v.at[at], mirror_out.at[at])
-        for at in (pl.ds(i * piece, piece) for i in range(in_s.shape[0] - 1))]
-    inward = [pltpu.make_async_copy(a, b, in_s.at[i]) for i, (a, b, _) in enumerate(views)]
-    outward = [pltpu.make_async_copy(b, c, out_s.at[i]) for i, (_, b, c) in enumerate(views)]
-    for copy in inward:
+def hand_over(new_in, mirror_in, new_out, mirror_out, sems):
+    copies = [
+        pltpu.make_async_copy(mirror_in, mirror_out, sems.at[0]),
+        pltpu.make_async_copy(new_in, new_out, sems.at[1]),
+    ]
+    for copy in copies:
         copy.start()
-    for first, then in zip(inward, outward):
-        first.wait()
-        then.start()
-    for copy in outward:
+    for copy in copies:
         copy.wait()
 
 
@@ -367,14 +356,15 @@
         tile_row, tile_col, source_rows, source_degree.reshape(-1, tile), edge_tiles, mirror_ids.reshape(-1, LANE),
         master_rows, master_degree.reshape(1, owned), weight_one, weight_two,
     )
+    operands = [pltpu.with_memory_space_constraint(a, pltpu.HBM) for a in operands]
     outs = pl.pallas_call(
         functools.partial(kernel, n_grp, n_mem),
         out_shape=(
-            jax.ShapeDtypeStruct((owned, width), bf),
-            jax.ShapeDtypeStruct((slot_total, width), bf),
+            pltpu.VMEM((owned, width), bf),
+            pltpu.VMEM((slot_total, width), bf),
         ),
         in_specs=[hbm] * len(operands),
-        out_specs=(hbm, hbm),
+        out_specs=(vmem, vmem),
         scratch_shapes=[
             pltpu.SMEM((n_tiles,), i32),
             pltpu.SMEM((n_tiles,), i32),
@@ -405,7 +395,6 @@
             pltpu.VMEM((HALVES, n_z, owned, LANE), bf),
             pltpu.VMEM((HALVES, PARTS, NX, rows, LANE), bf),
             pltpu.VMEM((HALVES, slot_total, LANE), bf),
-            pltpu.VMEM((owned, width), bf), dma((1 + HALVES,)),
             pltpu.SemaphoreType.REGULAR((n_z // 2 - 1,)), pltpu.SemaphoreType.REGULAR((n_z // 2 - 1,)),
             dma((len(operands) - 1,)), dma((FETCH,)),
             dma, dma,
@@ -417,16 +406,16 @@
             dma((HALVES,)), dma((HALVES,)),
         ],
         compiler_params=pltpu.CompilerParams(
-            collective_id=0, has_side_effects=True, vmem_limit_bytes=62 * 2**20),
+            collective_id=0, has_side_effects=True, vmem_limit_bytes=40 * 2**20),
         name="layer",
     )(*operands)
     return pl.pallas_call(
         hand_over,
         out_shape=tuple(jax.ShapeDtypeStruct(o.shape, o.dtype) for o in outs),
-        in_specs=[hbm, hbm],
+        in_specs=[vmem, vmem],
         out_specs=(hbm, hbm),
-        scratch_shapes=[pltpu.VMEM(o.shape, o.dtype) for o in outs] + [dma((5,)), dma((5,))],
-        compiler_params=pltpu.CompilerParams(vmem_limit_bytes=62 * 2**20),
+        scratch_shapes=[dma((2,))],
+        compiler_params=pltpu.CompilerParams(vmem_limit_bytes=16 * 2**20),
         name="hand_over",
     )(*outs)
 

time: 71.5 us -> 70.2 us (0.982)
  Pallas kernels: 70.4 us -> 69.3 us
    pallas_call x1, Pallas kernels: 1.85 us -> 0.81 us  [body(): pl.pallas_call(hand_over, out_shape=tuple((jax.ShapeDtypeStruct(o.shape,...]
where the time goes in v5:
time: 70.2 us; the launch traced here: 70.1 us
  Pallas kernels  69.3 us (99%)
  between operations  0.8 us (1%)
    pallas_call x1, Pallas kernels, body(): pl.pallas_call(functools.partial(kernel, n_grp, n_mem), out_shape=(pltpu....  68.5 us

profile of v5, /device:TPU:1, one launch (start us, length us, event | category | flops | bytes accessed | tf_op | source)
XLA Modules:
  0.0 70.1 jit_solution(4871169059214623645)
XLA Ops:
  0.6 68.5 %layer.1 = (bf16[32,256]{1,0:T(8,128)(2,1)S(1)}, bf16[1024,256]{1,0:T(8,128)(2,1)S(1)}) custom-call(s32[32]{0:T(128)} %trow_h.1, s32[32]{0:T(128)} %tcol_h.1, bf16[512,256]{1,0:T(8,128)(2,1)} %src_h.1, s32[4,128]{1,0:T(4,128)} %bitcast.4, s32[32,128,128]{2,1,0:T(8,128)} %tiles_h.1, s32[8,128]{1,0:T(8,128)} %bitcast.3, bf16[32,256]{1,0:T(8,128)(2,1)} %mrow_h.1, ...), custom_call_target="tpu_custom_call" | custom-call | tf_op jit(solution)/shard_map/layer/pallas_call | solution.py:360
  69.1 0.8 %hand_over.1 = (bf16[32,256]{1,0:T(8,128)(2,1)}, bf16[1024,256]{1,0:T(8,128)(2,1)}) custom-call(bf16[32,256]{1,0:T(8,128)(2,1)S(1)} %get-tuple-element.4.new_in, bf16[1024,256]{1,0:T(8,128)(2,1)S(1)} %get-tuple-element.5.mirror_in), custom_call_target="tpu_custom_call" | custom-call | tf_op jit(solution)/shard_map/hand_over/pallas_call | solution.py:412

commit v6 on v5

--- a/solution.py
+++ b/solution.py
@@ -85,29 +85,15 @@
     fetch[0].wait()
     fetch[1].wait()
     scale = lax.rsqrt(deg[...].astype(jnp.float32))
-    for k in range(src.shape[0] // tile):
-        column = jnp.broadcast_to(scale[k : k + 1, :], (tile, tile)).T
-        for h in range(HALVES):
+    columns = [
+        jnp.broadcast_to(scale[k : k + 1, :], (tile, tile)).T for k in range(src.shape[0] // tile)]
+    for copy in fetch[2:5]:
+        copy.wait()
+
+    def fill_rhs(h):
+        for k, column in enumerate(columns):
             at = (pl.ds(k * tile, tile), pl.ds(h * LANE, LANE))
             scaled[h, k] = (src[at].astype(jnp.float32) * column).astype(jnp.bfloat16)
-    for copy in fetch[2:5]:
-        copy.wait()
-
-    ids = idin[...]
-    group = jnp.right_shift(ids, log2(owned * n_mem))
-    dx = jnp.bitwise_and(group, NX - 1) - x
-    dx = jnp.where(dx < 0, dx + NX, dx)
-    dz = jnp.right_shift(group, log2(NX)) - z
-    dz = jnp.where(dz < 0, dz + n_z, dz)
-    order = 2 * jnp.abs(dz - half_z) - jnp.where(dz < half_z, 1, 0)
-    z_group = jnp.right_shift(order, log2(z_part))
-    spots = (z_group * NX + dx) * rows + jnp.bitwise_and(order, z_part - 1) * owned + jnp.bitwise_and(
-        ids, owned - 1)
-
-    for k in range(n_y):
-        place[k] = spots[k : k + 1, :]
-
-    def fill_rhs(h):
         for t in range(n_tiles):
             rhs[h, t * tile : (t + 1) * tile, :] = scaled[h, tcol[t]]
 
@@ -116,6 +102,21 @@
         fetch_tiles[i].wait()
         for t in range(i * step, (i + 1) * step):
             bits[t] = tiles[t].astype(jnp.float32).astype(jnp.bfloat16)
+
+    def find_places():
+        ids = idin[...]
+        group = jnp.right_shift(ids, log2(owned * n_mem))
+        dx = jnp.bitwise_and(group, NX - 1) - x
+        dx = jnp.where(dx < 0, dx + NX, dx)
+        dz = jnp.right_shift(group, log2(NX)) - z
+        dz = jnp.where(dz < 0, dz + n_z, dz)
+        order = 2 * jnp.abs(dz - half_z) - jnp.where(dz < half_z, 1, 0)
+        z_group = jnp.right_shift(order, log2(z_part))
+        spots = (z_group * NX + dx) * rows + jnp.bitwise_and(order, z_part - 1) * owned + jnp.bitwise_and(
+            ids, owned - 1)
+
+        for k in range(n_y):
+            place[k] = spots[k : k + 1, :]
 
     def sums_for(h, dy):
         block = lax.rem(y + dy, n_y)
@@ -187,7 +188,6 @@
         pltpu.make_async_copy(ref, ref, sem).wait()
 
     mine = pl.ds(pl.multiple_of(m * slots, slots), slots)
-    idrecv[0] = place[y]
     for h in range(HALVES):
         if h:
             fill_rhs(h)
@@ -201,12 +201,14 @@
             if h == 0 and i == 0:
                 tell(0)
             if h == 0 and i == 2:
+                find_places()
                 for d in mem_order:
                     id_copy(*d).start()
         precv[h, 0:slots] = part[h, 0, pl.ds(pl.multiple_of(c * slots, slots), slots), :]
 
     hear(0)
     drain(idrecv.at[pl.ds(1, n_mem - 1)], id_r)
+    idrecv[0] = place[y]
     for k in range(n_y):
         even[k : k + 1, :] = idrecv[NC * k]
         odd[k : k + 1, :] = idrecv[NC * k + 1]
@@ -227,6 +229,19 @@
     lax.fori_loop(0, n_table // LANE, build_put, 0)
 
     hear(1)
+
+    def rest_of_x(h, first, last):
+        for q in range(first, last):
+            drain(xrecv.at[h, q, pl.ds(1, NX - 1)], x_r.at[h, q])
+            total = xacc[h, q]
+            for j in range(1, NX):
+                total = total + xrecv[h, q, j].astype(jnp.float32)
+            xacc[h, q] = total
+            for i in range(z_part):
+                zsend[h, q * z_part + i] = total[i * owned : (i + 1) * owned].astype(jnp.bfloat16)
+            for k in z_order:
+                if pos(k) // z_part == q:
+                    z_copy(h, k).start()
 
     group_rows = NX * rows
     for h in range(HALVES):
@@ -240,19 +255,10 @@
         if h == 0:
             for r in range(2, half_z - 1):
                 hear(r)
-
-    for h in range(HALVES):
-        for q in range(PARTS):
-            drain(xrecv.at[h, q, pl.ds(1, NX - 1)], x_r.at[h, q])
-            total = xacc[h, q]
-            for j in range(1, NX):
-                total = total + xrecv[h, q, j].astype(jnp.float32)
-            xacc[h, q] = total
-            for i in range(z_part):
-                zsend[h, q * z_part + i] = total[i * owned : (i + 1) * owned].astype(jnp.bfloat16)
-            for k in z_order:
-                if pos(k) // z_part == q:
-                    z_copy(h, k).start()
+            rest_of_x(0, 0, PARTS // 3)
+
+    rest_of_x(0, PARTS // 3, PARTS)
+    rest_of_x(1, 0, PARTS)
 
     def build_take(k, carry):
         column = jnp.broadcast_to(even[pl.ds(k, 1), :], (LANE, LANE)).T
@@ -293,7 +299,7 @@
     for h in range(HALVES):
         table[h, own_q, 0, own_at, :] = new[:, h * LANE : (h + 1) * LANE]
 
-    for k in reversed(z_order):
+    for k in z_order[:3] + z_order[:2:-1]:
         gz_copy(0, k).start()
     newm[...] = new
     for h in range(HALVES):

time: 70.2 us -> 69.8 us (level)
  no operation moved by 1% of the time
where the time goes in v6:
time: 69.8 us; the launch traced here: 69.6 us
  Pallas kernels  68.8 us (99%)
  between operations  0.8 us (1%)
    pallas_call x1, Pallas kernels, body(): pl.pallas_call(functools.partial(kernel, n_grp, n_mem), out_shape=(pltpu....  68 us

profile of v6, /device:TPU:1, one launch (start us, length us, event | category | flops | bytes accessed | tf_op | source)
XLA Modules:
  0.0 69.6 jit_solution(4397391294325451571)
XLA Ops:
  0.6 68.0 %layer.1 = (bf16[32,256]{1,0:T(8,128)(2,1)S(1)}, bf16[1024,256]{1,0:T(8,128)(2,1)S(1)}) custom-call(s32[32]{0:T(128)} %trow_h.1, s32[32]{0:T(128)} %tcol_h.1, bf16[512,256]{1,0:T(8,128)(2,1)} %src_h.1, s32[4,128]{1,0:T(4,128)} %bitcast.4, s32[32,128,128]{2,1,0:T(8,128)} %tiles_h.1, s32[8,128]{1,0:T(8,128)} %bitcast.3, bf16[32,256]{1,0:T(8,128)(2,1)} %mrow_h.1, ...), custom_call_target="tpu_custom_call" | custom-call | tf_op jit(solution)/shard_map/layer/pallas_call | solution.py:366
  68.7 0.8 %hand_over.1 = (bf16[32,256]{1,0:T(8,128)(2,1)}, bf16[1024,256]{1,0:T(8,128)(2,1)}) custom-call(bf16[32,256]{1,0:T(8,128)(2,1)S(1)} %get-tuple-element.4.new_in, bf16[1024,256]{1,0:T(8,128)(2,1)S(1)} %get-tuple-element.5.mirror_in), custom_call_target="tpu_custom_call" | custom-call | tf_op jit(solution)/shard_map/hand_over/pallas_call | solution.py:418

commit v7 on v6

--- a/solution.py
+++ b/solution.py
@@ -55,6 +55,7 @@
 
     y_order = [0] + [s for d in range(1, n_y // 2) for s in (n_y - d, d)] + [n_y // 2]
     mem_order = [(dy, dc) for dy in reversed(y_order) for dc in range(NC) if (dy, dc) != (0, 0)]
+    near = (1, n_y - 1, 0)
     x_order = sorted(range(1, NX), key=lambda j: -min(j, NX - j))
     z_order = sorted(range(1, n_z), key=pos)
 
@@ -69,18 +70,14 @@
         pltpu.make_async_copy(tiles_h.at[pl.ds(i * step, step)], tiles.at[pl.ds(i * step, step)], tile_s.at[i])
         for i in range(FETCH)
     ]
-    for copy in fetch[:5]:
-        copy.start()
-    for copy in fetch_tiles:
-        copy.start()
-    for copy in fetch[5:]:
-        copy.start()
-
     barrier = pltpu.get_barrier_semaphore()
     partners = [(g, mem_of(*d)) for d in mem_order] + [(grp_x(j), m) for j in x_order] + [
         (grp_z(k), m) for k in (1, n_z - 1)]
     for who in partners:
         pl.semaphore_signal(barrier, inc=1, device_id=who, device_id_type=MESH)
+
+    for copy in fetch[:2] + fetch_tiles + fetch[2:]:
+        copy.start()
 
     fetch[0].wait()
     fetch[1].wait()
@@ -196,7 +193,7 @@
             if h == 0 and i == 0:
                 pl.semaphore_wait(barrier, len(partners))
             for dc in range(NC):
-                if (dy, dc) != (0, 0):
+                if (dy, dc) in mem_order and not (h and dy in near):
                     y_copy(h, dy, dc).start()
             if h == 0 and i == 0:
                 tell(0)
@@ -246,6 +243,10 @@
     group_rows = NX * rows
     for h in range(HALVES):
         drain(precv.at[h, pl.ds(slots, slot_total - slots)], y_r.at[h])
+        if h == 0:
+            for d in mem_order:
+                if d[0] in near:
+                    y_copy(1, *d).start()
         for q in range(PARTS):
             block = jnp.dot(put[q * group_rows : (q + 1) * group_rows, :], precv[h], preferred_element_type=jnp.float32)
             for j in x_order:
@@ -320,9 +321,14 @@
                 take[at, :], table[h].reshape(n_table, LANE), preferred_element_type=jnp.float32
             ).astype(jnp.bfloat16)
             for d in mem_order:
-                if d[0] // 2 * 2 == first:
+                if d[0] // 2 * 2 == first and d[0] not in near:
                     b_copy(h, *d).start()
         mirror[mine, h * LANE : (h + 1) * LANE] = served[h, 0:slots, :]
+
+    for h in range(HALVES):
+        for d in mem_order:
+            if d[0] in near:
+                b_copy(h, *d).start()
 
     drain(zrecv.at[:, pl.ds(1, n_z - 1)], gz_s)
     for h in range(HALVES):

time: 69.8 us -> 69.8 us (level)
  no operation moved by 1% of the time
where the time goes in v7:
time: 69.8 us; the launch traced here: 69.6 us
  Pallas kernels  68.8 us (99%)
  between operations  0.8 us (1%)
    pallas_call x1, Pallas kernels, body(): pl.pallas_call(functools.partial(kernel, n_grp, n_mem), out_shape=(pltpu....  68 us

profile of v7, /device:TPU:1, one launch (start us, length us, event | category | flops | bytes accessed | tf_op | source)
XLA Modules:
  0.0 69.6 jit_solution(13632111359922614677)
XLA Ops:
  0.6 68.0 %layer.1 = (bf16[32,256]{1,0:T(8,128)(2,1)S(1)}, bf16[1024,256]{1,0:T(8,128)(2,1)S(1)}) custom-call(s32[32]{0:T(128)} %trow_h.1, s32[32]{0:T(128)} %tcol_h.1, bf16[512,256]{1,0:T(8,128)(2,1)} %src_h.1, s32[4,128]{1,0:T(4,128)} %bitcast.4, s32[32,128,128]{2,1,0:T(8,128)} %tiles_h.1, s32[8,128]{1,0:T(8,128)} %bitcast.3, bf16[32,256]{1,0:T(8,128)(2,1)} %mrow_h.1, ...), custom_call_target="tpu_custom_call" | custom-call | tf_op jit(solution)/shard_map/layer/pallas_call | solution.py:372
  68.7 0.8 %hand_over.1 = (bf16[32,256]{1,0:T(8,128)(2,1)}, bf16[1024,256]{1,0:T(8,128)(2,1)}) custom-call(bf16[32,256]{1,0:T(8,128)(2,1)S(1)} %get-tuple-element.4.new_in, bf16[1024,256]{1,0:T(8,128)(2,1)S(1)} %get-tuple-element.5.mirror_in), custom_call_target="tpu_custom_call" | custom-call | tf_op jit(solution)/shard_map/hand_over/pallas_call | solution.py:424

commit v8 on v7

--- a/solution.py
+++ b/solution.py
@@ -73,10 +73,16 @@
     barrier = pltpu.get_barrier_semaphore()
     partners = [(g, mem_of(*d)) for d in mem_order] + [(grp_x(j), m) for j in x_order] + [
         (grp_z(k), m) for k in (1, n_z - 1)]
-    for who in partners:
-        pl.semaphore_signal(barrier, inc=1, device_id=who, device_id_type=MESH)
-
-    for copy in fetch[:2] + fetch_tiles + fetch[2:]:
+    def greet(some):
+        for who in some:
+            pl.semaphore_signal(barrier, inc=1, device_id=who, device_id_type=MESH)
+
+    far = NC * (n_y // 2 - 1)
+    greet(partners[:far])
+    for copy in fetch[:2] + fetch_tiles + fetch[2:5]:
+        copy.start()
+    greet(partners[far:])
+    for copy in fetch[5:]:
         copy.start()
 
     fetch[0].wait()
@@ -94,11 +100,24 @@
         for t in range(n_tiles):
             rhs[h, t * tile : (t + 1) * tile, :] = scaled[h, tcol[t]]
 
+    def fill_lhs(dy, tiles_here):
+        block = lax.rem(y + dy, n_y)
+        for t in tiles_here:
+            edges = bits[t]
+            lhs[dy, :, t * tile : (t + 1) * tile] = jnp.where(trow[t] == block, edges, jnp.zeros_like(edges))
+
     fill_rhs(0)
+    farthest, total = y_order[-1], None
     for i in range(FETCH):
         fetch_tiles[i].wait()
-        for t in range(i * step, (i + 1) * step):
+        here = range(i * step, (i + 1) * step)
+        for t in here:
             bits[t] = tiles[t].astype(jnp.float32).astype(jnp.bfloat16)
+        fill_lhs(farthest, here)
+        deep = slice(i * step * tile, (i + 1) * step * tile)
+        product = jnp.dot(lhs[farthest, :, deep], rhs[0, deep], preferred_element_type=jnp.float32)
+        total = product if total is None else total + product
+    part[0, farthest] = total.astype(jnp.bfloat16)
 
     def find_places():
         ids = idin[...]
@@ -116,13 +135,10 @@
             place[k] = spots[k : k + 1, :]
 
     def sums_for(h, dy):
-        block = lax.rem(y + dy, n_y)
-        if h == 0:
-            for t in range(n_tiles):
-                edges = bits[t]
-                lhs[dy, :, t * tile : (t + 1) * tile] = jnp.where(trow[t] == block, edges, jnp.zeros_like(edges))
-        part[h, dy] = jnp.dot(lhs[dy], rhs[h], preferred_element_type=jnp.float32).astype(jnp.bfloat16)
-
+        if (h, dy) != (0, farthest):
+            if h == 0:
+                fill_lhs(dy, range(n_tiles))
+            part[h, dy] = jnp.dot(lhs[dy], rhs[h], preferred_element_type=jnp.float32).astype(jnp.bfloat16)
 
     def slot_of(dy, dc):
         return dy * NC + dc

time: 69.8 us -> 70 us (level)
  no operation moved by 1% of the time
where the time goes in v8:
time: 70 us; the launch traced here: 69.8 us
  Pallas kernels  69 us (99%)
  between operations  0.8 us (1%)
    pallas_call x1, Pallas kernels, body(): pl.pallas_call(functools.partial(kernel, n_grp, n_mem), out_shape=(pltpu....  68.2 us

profile of v8, /device:TPU:1, one launch (start us, length us, event | category | flops | bytes accessed | tf_op | source)
XLA Modules:
  0.0 69.8 jit_solution(6593979860225338259)
XLA Ops:
  0.6 68.2 %layer.1 = (bf16[32,256]{1,0:T(8,128)(2,1)S(1)}, bf16[1024,256]{1,0:T(8,128)(2,1)S(1)}) custom-call(s32[32]{0:T(128)} %trow_h.1, s32[32]{0:T(128)} %tcol_h.1, bf16[512,256]{1,0:T(8,128)(2,1)} %src_h.1, s32[4,128]{1,0:T(4,128)} %bitcast.4, s32[32,128,128]{2,1,0:T(8,128)} %tiles_h.1, s32[8,128]{1,0:T(8,128)} %bitcast.3, bf16[32,256]{1,0:T(8,128)(2,1)} %mrow_h.1, ...), custom_call_target="tpu_custom_call" | custom-call | tf_op jit(solution)/shard_map/layer/pallas_call | solution.py:388
  68.8 0.8 %hand_over.1 = (bf16[32,256]{1,0:T(8,128)(2,1)}, bf16[1024,256]{1,0:T(8,128)(2,1)}) custom-call(bf16[32,256]{1,0:T(8,128)(2,1)S(1)} %get-tuple-element.4.new_in, bf16[1024,256]{1,0:T(8,128)(2,1)S(1)} %get-tuple-element.5.mirror_in), custom_call_target="tpu_custom_call" | custom-call | tf_op jit(solution)/shard_map/hand_over/pallas_call | solution.py:440
